TPU v7x, 32 devices: a whole 2x2x4 slice. The times are simulated.
32 devices in a mesh: mp: 2 (over core), feat: 16 (over z, y, x).
Axes of the slice: x: 2, y: 2, z: 4, core: 2. Of those that a mesh axis runs over, the one named last changes fastest.
Arguments:
- target_ids: int32 [16], replicated, may hold values from 0 to 127999
- target_pos: int32 [16], replicated, may hold values from 24 to 47
- unembed: bfloat16 [128000, 2304], P(('mp', 'feat')), may hold values from -6 to 6
- attn_weights: float32 [8, 16, 48, 48], P('mp'), may hold values from 0.02 to 1
- inv_rms: float32 [16, 48], replicated, may hold values from 0.5 to 2
- norm_gain: float32 [2304], replicated, may hold values from 0.1 to 1.9
- w_value: bfloat16 [4, 2304, 256], P(None, 'mp'), may hold values from -0.125 to 0.125
- w_out: bfloat16 [8, 256, 2304], P('mp'), may hold values from -0.375 to 0.375
- decoder: bfloat16 [2, 98304, 2304], P(None, ('mp', 'feat')), may hold values from -0.125 to 0.125
- activation: bfloat16 [16, 48, 98304], P(None, None, ('mp', 'feat')), may hold values from 0.5 to 4
- active: int32 [16, 48, 98304], P(None, None, ('mp', 'feat')), may hold values 0 or 1
Outputs:
- attribution: float32 [16, 48, 98304], P(None, None, ('mp', 'feat'))
All inputs are finite; a program needn't handle non-finite values. No bound on the sum of `active` on one device may be relied on, other than what follows from the above.
Results may differ from a plain program's by a relative error of at most 0.0035.
Values may be sent and summed in bfloat16 or wider, within the bound.
A program may use at most 128 MiB of HBM per device.

v0:
```python
import jax
import jax.numpy as jnp
from jax import lax
from jax.sharding import PartitionSpec as P


def on_device(
    target_ids,
    target_pos,
    unembed,
    attn_weights,
    inv_rms,
    norm_gain,
    w_value,
    w_out,
    decoder,
    activation,
    active,
):
    vocab_rows = unembed.shape[0]
    model_width = unembed.shape[1]
    targets = target_ids.shape[0]
    positions = inv_rms.shape[1]
    local_heads = w_out.shape[0]
    kv_heads = w_value.shape[0]
    column_count = w_value.shape[1]
    row_count = targets * positions
    own_rows = row_count // lax.axis_size("feat")
    device_rank = lax.axis_index("mp") * lax.axis_size("feat") + lax.axis_index("feat")
    first_row = device_rank * vocab_rows
    picker = (
        target_ids[:, None] == first_row + jnp.arange(vocab_rows, dtype=jnp.int32)[None, :]
    ).astype(jnp.bfloat16)
    direction = lax.psum(
        jnp.dot(picker, unembed, preferred_element_type=jnp.float32), ("mp", "feat")
    )
    placing = (jnp.arange(positions, dtype=jnp.int32)[None, :] == target_pos[:, None]).astype(
        jnp.float32
    )
    upper = (placing[:, :, None] * direction[:, None, :]).reshape(row_count, model_width)
    lowered_top = upper.astype(jnp.bfloat16)
    row_start = lax.axis_index("feat") * own_rows
    column_start = lax.axis_index("mp") * column_count
    index_pos = jnp.arange(positions, dtype=jnp.int32)
    causal = (index_pos[:, None] >= index_pos[None, :]).astype(jnp.float32)
    weights = attn_weights * causal
    pattern = weights / jnp.sum(weights, axis=-1, keepdims=True)
    flipped = jnp.swapaxes(pattern, 2, 3).reshape(local_heads, row_count, positions)
    own_pattern = lax.dynamic_slice_in_dim(flipped, row_start, own_rows, 1)
    row_group = (row_start + jnp.arange(own_rows, dtype=jnp.int32)) // positions
    group_pick = (row_group[:, None] == jnp.arange(targets, dtype=jnp.int32)[None, :]).astype(
        jnp.float32
    )
    block_pattern = (own_pattern[:, :, None, :] * group_pick[None, :, :, None]).reshape(
        local_heads, own_rows, row_count
    )
    mixed = jnp.einsum(
        "hrq,qd->hrd",
        block_pattern,
        lowered_top.astype(jnp.float32),
        precision=lax.Precision.HIGHEST,
    ).astype(jnp.bfloat16)
    spread = jnp.einsum("hrd,hkd->hrk", mixed, w_out, preferred_element_type=jnp.float32).astype(
        jnp.bfloat16
    )
    all_spread = lax.all_gather(spread, "mp", axis=0, tiled=True)
    group_size = local_heads * lax.axis_size("mp") // kv_heads
    value_heads = jnp.repeat(w_value, group_size, axis=0)
    heads_sum = jnp.einsum(
        "hrk,hck->rc", all_spread, value_heads, preferred_element_type=jnp.float32
    )
    upper_rows = lax.dynamic_slice_in_dim(upper, row_start, own_rows, 0)
    upper_block = lax.dynamic_slice_in_dim(upper_rows, column_start, column_count, 1)
    scale_rows = lax.dynamic_slice_in_dim(inv_rms.reshape(row_count, 1), row_start, own_rows, 0)
    gain_columns = lax.dynamic_slice_in_dim(norm_gain, column_start, column_count, 0)
    below_block = upper_block + scale_rows * gain_columns[None, :] * heads_sum
    lowered_block = below_block.astype(jnp.bfloat16)
    top_scores = jnp.einsum(
        "rd,fd->rf", lowered_top, decoder[1], preferred_element_type=jnp.float32
    )
    tall_block = lax.all_gather(lowered_block, "feat", axis=0, tiled=True)
    lowered_bottom = lax.all_gather(tall_block, "mp", axis=1, tiled=True)
    bottom_scores = jnp.einsum(
        "rd,fd->rf", lowered_bottom, decoder[0], preferred_element_type=jnp.float32
    )
    scores = bottom_scores + top_scores
    feature_count = decoder.shape[1]
    attribution = (
        activation.astype(jnp.float32).reshape(row_count, feature_count)
        * active.reshape(row_count, feature_count).astype(jnp.float32)
        * scores
    )
    return attribution.reshape(targets, positions, feature_count)


def solution(mesh):
    in_specs = (
        P(),
        P(),
        P(("mp", "feat"), None),
        P("mp", None, None, None),
        P(),
        P(),
        P(None, "mp", None),
        P("mp", None, None),
        P(None, ("mp", "feat"), None),
        P(None, None, ("mp", "feat")),
        P(None, None, ("mp", "feat")),
    )
    out_specs = P(None, None, ("mp", "feat"))
    return jax.shard_map(
        on_device, mesh=mesh, in_specs=in_specs, out_specs=out_specs, check_vma=False
    )
```

profile of v0, /device:TPU:0, one launch (start us, length us, event | category | flops | bytes accessed | tf_op | source)
XLA Modules:
  0.0 259.4 jit_solution(16619177516424895252)
XLA Ops:
  6.5 0.0 copy-start
  6.5 0.0 all-reduce.2.cloned.1.call-start
  6.5 0.0 copy-start.3
  6.6 0.0 copy-start.4
  6.6 0.0 copy-start.5
  6.6 9.6 %fusion.21 = f32[16,2304]{1,0:T(8,128)} fusion(bf16[4000,2304]{1,0:T(8,128)(2,1)} %param.13, s32[4000]{0:T(1024)S(1)} %iota_add_fusion, s32[16]{0:T(128)} %param.11), kind=kOutput, calls=%fused_computation.26 | convolution fusion | flops 294976000 | bytes 18595520 | tf_op jit(solution)/shard_map/dot_general | solution.py:35
  16.2 0.0 all-reduce.2.cloned.1.call-update
  16.2 0.0 all-gather.3.cloned.1.call-start
  16.3 0.0 copy-done.3
  16.3 0.1 reshape.146
  16.4 0.0 copy-done.4
  16.4 0.1 dynamic_slice.15
  16.5 0.0 copy-done.5
  16.5 0.1 fusion.26
  16.6 0.1 reshape.150
  16.7 1.9 fusion.16
  18.6 1.6 copy.14
  20.2 2.1 reshape.147
  22.3 0.1 constant_dynamic-slice_fusion
  22.4 0.1 copy.15
  22.5 0.1 dynamic-slice
  22.5 0.1 dynamic-slice_bitcast_fusion
  22.6 117.2 %all-reduce.2.cloned.1.call-done = f32[16,2304]{1,0:T(8,128)} async-done(((f32[16,2304]{1,0:T(8,128)}), f32[16,2304]{1,0:T(8,128)}) %all-reduce.2.cloned.1.call-update) | async-done | bytes 147472 | tf_op jit(solution)/shard_map/psum | solution.py:34
  139.8 4.2 %fusion.9 = bf16[4,48,2304]{2,1,0:T(8,128)(2,1)S(1)} fusion(f32[48,16]{0,1:T(8,128)S(1)} %fusion.27, f32[4,48,48]{2,1,0:T(8,128)S(1)} %copy.15, f32[16,48]{1,0:T(8,128)S(1)} %fusion.26, f32[16,2304]{1,0:T(8,128)} %all-reduce.2.cloned.1.call-done), kind=kOutput, calls=%fused_computation.11 | convolution fusion | flops 4080992256 | bytes 1075200 | tf_op jit(solution)/shard_map/hrq,qd->hrd/dot_general | solution.py:57
  144.0 3.8 %convolution_convert_fusion = bf16[4,48,256]{2,1,0:T(8,128)(2,1)S(1)} fusion(bf16[4,48,2304]{2,1,0:T(8,128)(2,1)S(1)} %fusion.9, bf16[4,256,2304]{2,1,0:T(8,128)(2,1)} %param.18), kind=kOutput, calls=%fused_computation.22 | convolution fusion | flops 226541568 | bytes 5701632 | tf_op jit(solution)/shard_map/hrd,hkd->hrk/dot_general | solution.py:63
  147.8 0.0 copy-start.2
  147.8 2.9 %all_gather.9 = bf16[8,48,256]{2,1,0:T(8,128)(2,1)S(1)} all-gather(bf16[4,48,256]{2,1,0:T(8,128)(2,1)S(1)} %convolution_convert_fusion), channel_id=1, replica_groups=mesh['mp'=2,'feat'=16] {'mp'}, dimensions={0}, use_global_device_ids=true | all-gather | bytes 294912 | tf_op jit(solution)/shard_map/all_gather | solution.py:66
  150.8 0.0 copy-done
  150.8 0.3 broadcast_in_dim.2
  151.1 0.0 copy-done.2
  151.1 0.5 mul.95
  151.6 2.1 fusion.13
  153.8 0.0 all-gather.3.cloned.1.call-update
  153.8 0.2 all-gather.5.cloned.1.call-start
  154.0 11.0 %convert_multiply_fusion = f32[16,48,3072]{2,1,0:T(8,128)} fusion(s32[16,48,3072]{2,1,0:T(8,128)} %param.21, bf16[16,48,3072]{2,1,0:T(8,128)(2,1)} %param.20), kind=kLoop, calls=%fused_computation.8 | loop fusion | flops 7077888 | bytes 23592960 | tf_op jit(solution)/shard_map/mul | solution.py:89
  165.0 49.0 %all-gather.3.cloned.1.call-done = bf16[768,1152]{1,0:T(8,128)(2,1)} async-done(((bf16[48,1152]{1,0:T(8,128)(2,1)}), bf16[768,1152]{1,0:T(8,128)(2,1)}) %all-gather.3.cloned.1.call-update) | async-done | bytes 1769488 | tf_op jit(solution)/shard_map/all_gather | solution.py:81
  214.0 0.0 all-gather.5.cloned.1.call-update
  214.0 0.5 multiply_convert_fusion
  214.5 16.5 %fusion.1 = f32[768,3072]{1,0:T(8,128)} fusion(bf16[768,2304]{1,0:T(8,128)(2,1)S(1)} %bitcast.47, bf16[2,3072,2304]{2,1,0:T(8,128)(2,1)} %param.19), kind=kOutput, calls=%fused_computation.1 | convolution fusion | flops 10871635968 | bytes 27131904 | tf_op jit(solution)/shard_map/rd,fd->rf/dot_general | solution.py:78
  231.1 0.0 all-gather.5.cloned.1.call-done
  231.1 0.0 copy-start.1
  231.1 21.8 %bitcast_multiply_fusion = f32[768,3072]{1,0:T(8,128)} fusion(f32[16,48,3072]{2,1,0:T(8,128)} %convert_multiply_fusion, f32[768,3072]{1,0:T(8,128)} %fusion.1, bf16[768,2304]{1,0:T(8,128)(2,1)} %all-gather.5.cloned.1.call-done, bf16[2,3072,2304]{2,1,0:T(8,128)(2,1)} %param.19), kind=kOutput, calls=%fused_computation.7 | convolution fusion | flops 10876354560 | bytes 46006272 | tf_op jit(solution)/shard_map/rd,fd->rf/dot_general | solution.py:83
  252.9 0.0 copy-done.1
  (4 shorter events, 0.0 us)
Async XLA Ops:
  6.5 144.2 %copy-start = (bf16[4,1152,256]{2,1,0:T(8,128)(2,1)S(1)}, bf16[4,1152,256]{2,1,0:T(8,128)(2,1)}, u32[]{:S(2)}) copy-start(bf16[4,1152,256]{2,1,0:T(8,128)(2,1)} %param.17) | copy-start | bytes 7077892
  6.5 133.3 %all-reduce.2.cloned.1.call-start = ((), (), s32[]{:S(2)}) async-start(), calls=%async_computation | async-start | bytes 294912 | tf_op jit(solution)/shard_map/psum | solution.py:34
  6.5 9.8 %copy-start.3 = (f32[16,48]{1,0:T(8,128)S(1)}, f32[16,48]{1,0:T(8,128)}, u32[]{:S(2)}) copy-start(f32[16,48]{1,0:T(8,128)} %param.15) | copy-start | bytes 9220
  6.6 9.9 %copy-start.4 = (f32[2304]{0:T(1024)S(1)}, f32[2304]{0:T(1024)}, u32[]{:S(2)}) copy-start(f32[2304]{0:T(1024)} %param.16) | copy-start | bytes 27652
  6.6 9.9 %copy-start.5 = (s32[16]{0:T(128)S(1)}, s32[16]{0:T(128)}, u32[]{:S(2)}) copy-start(s32[16]{0:T(128)} %param.12) | copy-start | bytes 196
  16.2 197.8 %all-gather.3.cloned.1.call-start = ((), (), s32[]{:S(2)}) async-start(), calls=%async_computation.1 | async-start | bytes 1880064 | tf_op jit(solution)/shard_map/all_gather | solution.py:81
  147.8 3.3 %copy-start.2 = (f32[16,2304]{1,0:T(8,128)S(1)}, f32[16,2304]{1,0:T(8,128)}, u32[]{:S(2)}) copy-start(f32[16,2304]{1,0:T(8,128)} %all-reduce.2.cloned.1.call-done) | copy-start | bytes 442372
  153.8 77.3 %all-gather.5.cloned.1.call-start = ((), (), s32[]{:S(2)}) async-start(), calls=%async_computation.2 | async-start | bytes 5308416 | tf_op jit(solution)/shard_map/all_gather | solution.py:82
  231.1 21.8 %copy-start.1 = (bf16[4,1152,256]{2,1,0:T(8,128)(2,1)S(1)}, bf16[4,1152,256]{2,1,0:T(8,128)(2,1)}, u32[]{:S(2)}) copy-start(bf16[4,1152,256]{2,1,0:T(8,128)(2,1)} %param.17) | copy-start | bytes 7077892
Sparse Core Ops, SparseCore 0:
  16.3 123.4 all-reduce.1
  153.9 60.0 all-gather.2
  215.5 11.4 all-gather.4
where the time goes:
time: 260 us; the launch traced here: 259 us
  waiting for transfers between devices  166 us (64%)
  matrix products  58.1 us (22%)
  other arithmetic  13.5 us (5%)
  between operations  13.3 us (5%)
  local copies, waits for them, and re-layouts  5.13 us (2%)
  blocking collectives  2.93 us (1%)
    psum x1, waiting for transfers between devices, on_device(): lax.psum(jnp.dot(picker, unembed, preferred_element_type=jnp.float32), ('...  117 us
    all_gather x1, waiting for transfers between devices, on_device(): tall_block = lax.all_gather(lowered_block, 'feat', axis=0, tiled=True)  49 us
    dot_general x1, matrix products, on_device(): jnp.einsum('rd,fd->rf', lowered_bottom, decoder[0], preferred_element_typ...  21.8 us
    dot_general x1, matrix products, on_device(): jnp.einsum('rd,fd->rf', lowered_top, decoder[1], preferred_element_type=j...  16.5 us
    mul x1, other arithmetic, on_device(): activation.astype(jnp.float32).reshape(row_count, feature_count)  11 us
    dot_general x1, matrix products, on_device(): jnp.dot(picker, unembed, preferred_element_type=jnp.float32)  9.62 us
  transfers between devices with their start and end apart: 3, of which 2 were waited for; matrix products, arithmetic and copies ran while one was open for 13% of the time, Pallas kernels for 0%

commit v1 on v0

v1 whole, which is shorter than its diff:
```python
import functools

import jax
import jax.numpy as jnp
from jax import lax
from jax.experimental import pallas as pl
from jax.experimental.pallas import tpu as pltpu
from jax.sharding import PartitionSpec as P

MESH = pl.DeviceIdType.MESH
NT = (((1,), (1,)), ((), ()))
TILE = 16


def bits_of(n):
    return [1 << b for b in range(n.bit_length() - 1)]


def flip(index, bit):
    return index + bit - 2 * bit * lax.rem(lax.div(index, bit), 2)


def chunk_of(n, most):
    return max(c for c in range(TILE, most + 1, TILE) if n % c == 0)


def pick_kernel(ids, unembed, dir_ref, blocks, sems):
    rows, width = unembed.shape
    targets = dir_ref.shape[1]
    half = width // 2
    rank = lax.axis_index("mp") * lax.axis_size("feat") + lax.axis_index("feat")
    first = rank * rows

    def fetch(g):
        local = jnp.clip(ids[g] - first, 0, rows - 1)
        base = pl.multiple_of(lax.div(local, TILE) * TILE, TILE)
        return pltpu.make_async_copy(
            unembed.at[pl.ds(base, TILE), :],
            blocks.at[pl.ds(g * TILE, TILE), :],
            sems.at[g],
        )

    for g in range(targets):
        fetch(g).start()
    lane = lax.broadcasted_iota(jnp.int32, (targets, targets * TILE), 1)
    row = lax.broadcasted_iota(jnp.int32, (targets, targets * TILE), 0)
    picker = jnp.zeros((targets, targets * TILE), jnp.float32)
    for g in range(targets):
        local = ids[g] - first
        inside = (local >= 0) & (local < rows)
        at = jnp.where(inside, g * TILE + lax.rem(jnp.maximum(local, 0), TILE), -1)
        picker = jnp.where((row == g) & (lane == at), 1.0, picker)
    for g in range(targets):
        fetch(g).wait()
    picker = picker.astype(jnp.bfloat16)
    for c in range(2):
        dir_ref[c] = jnp.dot(
            picker, blocks[:, pl.ds(c * half, half)], preferred_element_type=jnp.float32
        ).astype(jnp.bfloat16)


def place_coefficients(pos, attn, inv_rms, ct_ref):
    heads, targets, positions, _ = attn.shape
    total = targets * positions
    spots = lax.broadcasted_iota(jnp.int32, (positions, total), 1) - lax.broadcasted_iota(
        jnp.int32, (positions, total), 0
    )
    tile = jnp.zeros((positions, total), jnp.float32)
    for g in range(targets):
        tile = jnp.where(spots == g * positions, 1.0, tile)
    lane = lax.broadcasted_iota(jnp.int32, (targets, total), 1)
    row = lax.broadcasted_iota(jnp.int32, (targets, total), 0)
    own = (lane >= row * positions) & (lane < (row + 1) * positions)
    t_iota = lax.broadcasted_iota(jnp.int32, (positions, positions), 0)
    s_row = lax.broadcasted_iota(jnp.int32, (1, positions), 1)
    for h in range(heads):
        lines = []
        for g in range(targets):
            line = jnp.sum(
                jnp.where(t_iota == pos[g], attn[h, g], 0.0), axis=0, keepdims=True
            )
            lines.append(jnp.where(s_row <= pos[g], line, 0.0))
        weights = jnp.concatenate(lines, axis=0)
        pattern = weights / jnp.sum(weights, axis=-1, keepdims=True) * inv_rms[...]
        spreadout = jnp.dot(
            pattern, tile, precision=lax.Precision.HIGHEST, preferred_element_type=jnp.float32
        )
        ct_ref[pl.ds(h * targets, targets), :] = jnp.where(own, spreadout, 0.0).astype(
            jnp.bfloat16
        )


def target_rows(pos, targets, positions):
    total = targets * positions
    lane = lax.broadcasted_iota(jnp.int32, (targets, total), 1)
    row = lax.broadcasted_iota(jnp.int32, (targets, total), 0)
    delta = jnp.zeros((targets, total), jnp.float32)
    for g in range(targets):
        delta = jnp.where((row == g) & (lane == g * positions + pos[g]), 1.0, delta)
    return delta


def share_kernel(
    n_mp,
    n_feat,
    pos,
    dir_ref,
    attn,
    inv_rms,
    gain_ref,
    w_out,
    w_value,
    lower,
    c_ref,
    pair_in,
    acc,
    got,
    dir_full,
    attn_v,
    w_out_v,
    w_full,
    u_all,
    ct_own,
    ct_all,
    pair_sem,
    step_send,
    step_recv,
    full_sem,
    w_sem,
    gather_send,
    gather_recv,
):
    mp = lax.axis_index("mp")
    feat = lax.axis_index("feat")
    mine = lax.rem(mp, 2)
    other = 1 - mine
    pair = {"mp": flip(mp, 1)}
    stages = [("feat", b) for b in bits_of(n_feat)] + [("mp", b) for b in bits_of(n_mp)[1:]]
    count, pieces = len(stages), got.shape[1]
    targets = dir_ref.shape[1]
    half = dir_ref.shape[2]
    width = 2 * half
    local_heads = w_out.shape[0]
    kv_heads, columns, head_size = w_value.shape
    heads = local_heads * n_mp

    own_columns = pl.ds(pl.multiple_of(mp * columns, TILE), columns)
    load_attn = pltpu.make_async_copy(attn, attn_v, w_sem.at[2])
    load_out = pltpu.make_async_copy(w_out, w_out_v, w_sem.at[0])
    load_value = pltpu.make_async_copy(w_value, w_full.at[:, own_columns, :], w_sem.at[1])
    load_attn.start()
    load_out.start()
    load_value.start()

    def partner(stage):
        axis, bit = stages[stage]
        return {axis: flip(feat if axis == "feat" else mp, bit)}

    barrier = pltpu.get_barrier_semaphore()
    greeted = [{"feat": flip(feat, b)} for b in bits_of(n_feat)]
    greeted += [{"mp": lax.rem(mp + o, n_mp)} for o in range(1, n_mp)]
    for device in greeted:
        pl.semaphore_signal(barrier, inc=1, device_id=device, device_id_type=MESH)
    pl.semaphore_wait(barrier, len(greeted))

    def remote(src, dst, send, recv, device):
        copy = pltpu.make_async_remote_copy(
            src_ref=src,
            dst_ref=dst,
            send_sem=send,
            recv_sem=recv,
            device_id=device,
            device_id_type=MESH,
        )
        copy.start()
        return copy

    def gather(kind, src, dst):
        return [
            remote(
                src,
                dst,
                gather_send.at[kind, o - 1],
                gather_recv.at[kind, o - 1],
                {"mp": lax.rem(mp + o, n_mp)},
            )
            for o in range(1, n_mp)
        ]

    first = remote(dir_ref.at[other], pair_in, pair_sem.at[0], pair_sem.at[1], pair)
    values_sent = gather(0, w_value, w_full.at[:, own_columns, :])
    first.wait()
    start = dir_ref[mine] + pair_in[...]
    size = half // pieces
    for p in range(pieces):
        acc[0, p] = start[:, p * size : (p + 1) * size]
    coefficients_sent = []
    for k in range(count):
        copies = []
        for p in range(pieces):
            copies.append(
                remote(
                    acc.at[k, p],
                    got.at[k, p],
                    step_send.at[k, p],
                    step_recv.at[k, p],
                    partner((k + p) % count),
                )
            )
        if k == 0:
            load_attn.wait()
            place_coefficients(pos, attn_v, inv_rms, ct_own)
            coefficients_sent = gather(1, ct_own, ct_all.at[mp])
            ct_all[mp] = ct_own[...]
        for p in range(pieces):
            copies[p].wait()
            acc[k + 1, p] = acc[k, p] + got[k, p]
    for p in range(pieces):
        dir_full[mine, :, p * size : (p + 1) * size] = acc[count, p]
    last = remote(
        dir_full.at[mine], dir_full.at[mine], full_sem.at[0], full_sem.at[1], pair
    )
    load_out.wait()
    last.wait()

    for c in range(2):
        part = dir_full[c]
        lower[pl.ds(heads * targets, targets), pl.ds(c * half, half)] = part
        lower[pl.ds((heads + 1) * targets, targets), pl.ds(c * half, half)] = part
    direction = lower[pl.ds(heads * targets, targets), :]
    own_u = lax.dot_general(
        direction,
        w_out_v[...].reshape(local_heads * head_size, width),
        NT,
        preferred_element_type=jnp.float32,
    ).astype(jnp.bfloat16)
    for l in range(local_heads):
        u_all[mp, l] = own_u[:, l * head_size : (l + 1) * head_size]
    u_sent = gather(2, u_all.at[mp], u_all.at[mp])

    for copy in coefficients_sent:
        copy.wait()
    delta = target_rows(pos, targets, inv_rms.shape[1])
    coefficients = jnp.concatenate(
        [ct_all[m].astype(jnp.float32) for m in range(n_mp)] + [delta] * 2, axis=0
    )
    c_ref[...] = coefficients.T.astype(jnp.bfloat16)
    load_value.wait()
    for copy in values_sent:
        copy.wait()
    for copy in u_sent:
        copy.wait()
    group = heads // kv_heads
    gain = gain_ref[...].reshape(1, width)
    for kv in range(kv_heads):
        spread = jnp.concatenate(
            [
                u_all[h // local_heads, h % local_heads]
                for h in range(kv * group, (kv + 1) * group)
            ],
            axis=0,
        )
        value = lax.dot_general(spread, w_full[kv], NT, preferred_element_type=jnp.float32)
        lower[pl.ds(kv * group * targets, group * targets), :] = (value * gain).astype(
            jnp.bfloat16
        )


def gate_kernel(straight, c_ref, lower, dec, act_ref, on_ref, out_ref):
    rank_rows = lower.shape[0]
    top_row = rank_rows - straight
    bottom = lax.dot_general(dec[0], lower[...], NT, preferred_element_type=jnp.float32)
    top = lax.dot_general(
        dec[1], lower[pl.ds(top_row, straight), :], NT, preferred_element_type=jnp.float32
    )
    both = bottom[:, top_row:] + top
    high = both.astype(jnp.bfloat16).astype(jnp.float32)
    lane = lax.broadcasted_iota(jnp.int32, both.shape, 1)
    low = jnp.where(lane < straight // 2, high, both - high)
    z = jnp.concatenate([bottom[:, :top_row], low], axis=1).astype(jnp.bfloat16)
    scores = lax.dot_general(c_ref[...], z, NT, preferred_element_type=jnp.float32)
    out_ref[...] = act_ref[...].astype(jnp.float32) * on_ref[...].astype(jnp.float32) * scores


def on_device(
    n_mp,
    n_feat,
    target_ids,
    target_pos,
    unembed,
    attn_weights,
    inv_rms,
    norm_gain,
    w_value,
    w_out,
    decoder,
    activation,
    active,
):
    vocab_rows, width = unembed.shape
    targets, positions = inv_rms.shape
    local_heads = w_out.shape[0]
    kv_heads, columns, head_size = w_value.shape
    features = decoder.shape[1]
    total = targets * positions
    half = width // 2
    heads = local_heads * n_mp
    rank_rows = heads * targets + 2 * targets
    bf16, f32 = jnp.bfloat16, jnp.float32
    vmem = pl.BlockSpec(memory_space=pltpu.VMEM)
    smem = pl.BlockSpec(memory_space=pltpu.SMEM)
    hbm = pl.BlockSpec(memory_space=pl.ANY)

    if vocab_rows % TILE:
        unembed = jnp.pad(unembed, ((0, TILE - vocab_rows % TILE), (0, 0)))
        rank = lax.axis_index("mp") * n_feat + lax.axis_index("feat")
        local = target_ids - rank * vocab_rows
        inside = (local >= 0) & (local < vocab_rows)
        target_ids = jnp.where(inside, rank * unembed.shape[0] + local, -1)
    direction = pl.pallas_call(
        pick_kernel,
        out_shape=jax.ShapeDtypeStruct((2, targets, half), bf16),
        in_specs=[smem, hbm],
        out_specs=vmem,
        scratch_shapes=[
            pltpu.VMEM((targets * TILE, width), bf16),
            pltpu.SemaphoreType.DMA((targets,)),
        ],
        compiler_params=pltpu.CompilerParams(vmem_limit_bytes=63 * 2**20),
        cost_estimate=pl.CostEstimate(
            flops=2 * targets * targets * TILE * width,
            bytes_accessed=2 * targets * TILE * width,
            transcendentals=0,
        ),
        name="pick_rows",
    )(target_ids, unembed)

    steps = len(bits_of(n_feat)) + len(bits_of(n_mp)) - 1
    pieces = 3 if half % (3 * 128) == 0 else 1
    size = half // pieces
    dma = pltpu.SemaphoreType.DMA
    lower, c = pl.pallas_call(
        functools.partial(share_kernel, n_mp, n_feat),
        out_shape=(
            jax.ShapeDtypeStruct((rank_rows, width), bf16),
            jax.ShapeDtypeStruct((total, rank_rows), bf16),
        ),
        in_specs=[smem, vmem, hbm, vmem, vmem, hbm, hbm],
        out_specs=(vmem, vmem),
        scratch_shapes=[
            pltpu.VMEM((targets, half), bf16),
            pltpu.VMEM((steps + 1, pieces, targets, size), bf16),
            pltpu.VMEM((steps, pieces, targets, size), bf16),
            pltpu.VMEM((2, targets, half), bf16),
            pltpu.VMEM(attn_weights.shape, f32),
            pltpu.VMEM(w_out.shape, bf16),
            pltpu.VMEM((kv_heads, columns * n_mp, head_size), bf16),
            pltpu.VMEM((n_mp, local_heads, targets, head_size), bf16),
            pltpu.VMEM((local_heads * targets, total), bf16),
            pltpu.VMEM((n_mp, local_heads * targets, total), bf16),
            dma((2,)),
            dma((steps, pieces)),
            dma((steps, pieces)),
            dma((2,)),
            dma((3,)),
            dma((3, n_mp - 1)),
            dma((3, n_mp - 1)),
        ],
        compiler_params=pltpu.CompilerParams(
            collective_id=0, has_side_effects=True, vmem_limit_bytes=63 * 2**20
        ),
        cost_estimate=pl.CostEstimate(
            flops=2 * features * width * rank_rows,
            bytes_accessed=4 * features * width + 6 * total * features,
            transcendentals=0,
        ),
        name="share",
    )(target_pos, direction, attn_weights, inv_rms, norm_gain, w_out, w_value)

    chunk = chunk_of(features, 384)
    out = pl.pallas_call(
        functools.partial(gate_kernel, 2 * targets),
        grid=(features // chunk,),
        out_shape=jax.ShapeDtypeStruct((total, features), f32),
        in_specs=[
            pl.BlockSpec((total, rank_rows), lambda i: (0, 0)),
            pl.BlockSpec((rank_rows, width), lambda i: (0, 0)),
            pl.BlockSpec((2, chunk, width), lambda i: (0, i, 0)),
            pl.BlockSpec((total, chunk), lambda i: (0, i)),
            pl.BlockSpec((total, chunk), lambda i: (0, i)),
        ],
        out_specs=pl.BlockSpec((total, chunk), lambda i: (0, i)),
        compiler_params=pltpu.CompilerParams(vmem_limit_bytes=63 * 2**20),
        cost_estimate=pl.CostEstimate(
            flops=2 * features * (width + total) * rank_rows,
            bytes_accessed=10 * total * features + 4 * features * width,
            transcendentals=0,
        ),
        name="score_and_gate",
    )(c, lower, decoder, activation.reshape(total, features), active.reshape(total, features))
    return out.reshape(targets, positions, features)


def solution(mesh):
    in_specs = (
        P(),
        P(),
        P(("mp", "feat"), None),
        P("mp", None, None, None),
        P(),
        P(),
        P(None, "mp", None),
        P("mp", None, None),
        P(None, ("mp", "feat"), None),
        P(None, None, ("mp", "feat")),
        P(None, None, ("mp", "feat")),
    )
    out_specs = P(None, None, ("mp", "feat"))
    return jax.shard_map(
        functools.partial(on_device, mesh.shape["mp"], mesh.shape["feat"]),
        mesh=mesh,
        in_specs=in_specs,
        out_specs=out_specs,
        check_vma=False,
    )
```

time: 260 us -> 50.1 us (0.19)
  waiting for transfers between devices: 166 us -> 0 us
  matrix products: 58.1 us -> 0 us
  Pallas kernels: 0 us -> 49.9 us
  other arithmetic: 13.5 us -> 0 us
  between operations: 13.3 us -> 0.02 us
  local copies, waits for them, and re-layouts: 5.13 us -> 0 us
  blocking collectives: 2.93 us -> 0 us
    psum x1 -> x0, waiting for transfers between devices: 117 us -> none  [on_device(): lax.psum(jnp.dot(picker, unembed, preferred_element_type=jnp.float32), ('...]
    dot_general x6 -> x0, matrix products: 58.1 us -> none  [the longest x1 21.8 us: on_device(): jnp.einsum('rd,fd->rf', lowered_bottom, decoder[0], preferred_element_typ...]
    pallas_call x0 -> x3, Pallas kernels: none -> 49.9 us  [the longest x1 24.4 us: on_device(): pl.pallas_call(functools.partial(share_kernel, n_mp, n_feat), out_shape=(...]
    all_gather x2 -> x0, waiting for transfers between devices: 49 us -> none  [the longest x1 49 us: on_device(): tall_block = lax.all_gather(lowered_block, 'feat', axis=0, tiled=True)]
    mul x1 -> x0, other arithmetic: 11 us -> none  [on_device(): activation.astype(jnp.float32).reshape(row_count, feature_count)]
    all_gather x1 -> x0, blocking collectives: 2.93 us -> none  [on_device(): all_spread = lax.all_gather(spread, 'mp', axis=0, tiled=True)]
  transfers between devices with their start and end apart: 3 -> 0, of which waited for: 2 -> 0; matrix products, arithmetic and copies ran while one was open for 13% -> 0% of each run, Pallas kernels for 0% -> 0%
where the time goes in v1:
time: 50.1 us; the launch traced here: 49.9 us
  Pallas kernels  49.9 us (100%)
    pallas_call x1, Pallas kernels, on_device(): pl.pallas_call(functools.partial(share_kernel, n_mp, n_feat), out_shape=(...  24.4 us
    pallas_call x1, Pallas kernels, on_device(): pl.pallas_call(functools.partial(gate_kernel, 2 * targets), grid=(feature...  21.5 us
    pallas_call x1, Pallas kernels, on_device(): pl.pallas_call(pick_kernel, out_shape=jax.ShapeDtypeStruct((2, targets, h...  3.99 us

profile of v1, /device:TPU:0, one launch (start us, length us, event | category | flops | bytes accessed | tf_op | source)
XLA Modules:
  0.0 49.9 jit_solution(13385301889066642049)
XLA Ops:
  0.0 4.0 %pick_rows.1.dir_ref = bf16[2,16,1152]{2,1,0:T(8,128)(2,1)} custom-call(s32[16]{0:T(128)} %ids.1, bf16[4000,2304]{1,0:T(8,128)(2,1)} %unembed.1), custom_call_target="tpu_custom_call" | custom-call | flops 18874368 | bytes 1179648 | tf_op jit(solution)/shard_map/pick_rows/pallas_call | solution.py:320
  4.0 24.4 %share.1 = (bf16[160,2304]{1,0:T(8,128)(2,1)}, bf16[768,160]{1,0:T(8,128)(2,1)}) custom-call(s32[16]{0:T(128)} %pos.1, bf16[2,16,1152]{2,1,0:T(8,128)(2,1)} %pick_rows.1.dir_ref, f32[4,16,48,48]{3,2,1,0:T(8,128)} %attn.1, f32[16,48]{1,0:T(8,128)} %inv_rms.1, f32[2304]{0:T(1024)} %gain_ref.1, bf16[4,256,2304]{2,1,0:T(8,128)(2,1)} %w_out.1, ...), custom_call_target="tpu_custom_call" | custom-call | flops 2264924160 | bytes 42467328 | tf_op jit(solution)/shard_map/share/pallas_call | solution.py:342
  28.4 21.5 %score_and_gate.1 = f32[768,3072]{1,0:T(8,128)} custom-call(bf16[768,160]{1,0:T(8,128)(2,1)} %get-tuple-element.7.c_ref, bf16[160,2304]{1,0:T(8,128)(2,1)} %get-tuple-element.8.lower, bf16[2,3072,2304]{2,1,0:T(8,128)(2,1)} %dec.1, bf16[768,3072]{1,0:T(8,128)(2,1)} %bitcast.4, s32[768,3072]{1,0:T(8,128)} %bitcast.3), custom_call_target="tpu_custom_call" | custom-call | flops 3019898880 | bytes 51904512 | tf_op jit(solution)/shard_map/score_and_gate/pallas_call | solution.py:381

commit v2 on v1

--- a/solution.py
+++ b/solution.py
@@ -103,6 +103,7 @@
 def share_kernel(
     n_mp,
     n_feat,
+    chunk,
     pos,
     dir_ref,
     attn,
@@ -110,8 +111,18 @@
     gain_ref,
     w_out,
     w_value,
+    dec,
+    act,
+    on,
+    z_ref,
+    gate_ref,
+    c_ref,
     lower,
-    c_ref,
+    dec_v,
+    z_v,
+    act_v,
+    on_v,
+    gate_v,
     pair_in,
     acc,
     got,
@@ -129,6 +140,10 @@
     w_sem,
     gather_send,
     gather_recv,
+    dec_sem,
+    z_sem,
+    gate_in_sem,
+    gate_out_sem,
 ):
     mp = lax.axis_index("mp")
     feat = lax.axis_index("feat")
@@ -148,9 +163,59 @@
     load_attn = pltpu.make_async_copy(attn, attn_v, w_sem.at[2])
     load_out = pltpu.make_async_copy(w_out, w_out_v, w_sem.at[0])
     load_value = pltpu.make_async_copy(w_value, w_full.at[:, own_columns, :], w_sem.at[1])
-    load_attn.start()
     load_out.start()
     load_value.start()
+
+    features = dec.shape[1]
+    chunks = features // chunk
+    lines = gate_v.shape[1]
+    parts = act.shape[0] // lines
+    points = count + 2
+
+    def load_dec(layer, i):
+        at = pl.ds(pl.multiple_of(i * chunk, chunk), chunk)
+        return pltpu.make_async_copy(
+            dec.at[layer, at, :], dec_v.at[layer, at, :], dec_sem.at[layer, i]
+        )
+
+    def load_gate(j):
+        at = pl.ds(j * lines, lines)
+        return [
+            pltpu.make_async_copy(act.at[at, :], act_v.at[j % 2], gate_in_sem.at[0, j]),
+            pltpu.make_async_copy(on.at[at, :], on_v.at[j % 2], gate_in_sem.at[1, j]),
+        ]
+
+    def store_gate(j):
+        return pltpu.make_async_copy(
+            gate_v.at[j % 2], gate_ref.at[pl.ds(j * lines, lines), :], gate_out_sem.at[j]
+        )
+
+    for copy in load_gate(0):
+        copy.start()
+    each = -(-2 * chunks // points)
+
+    def beside(j):
+        if j + 1 < parts:
+            for copy in load_gate(j + 1):
+                copy.start()
+        for i in range(j * each, min((j + 1) * each, 2 * chunks)):
+            load_dec(i % 2, i // 2).start()
+        if j < parts:
+            for copy in load_gate(j):
+                copy.wait()
+            if j >= 2:
+                store_gate(j - 2).wait()
+
+            def multiply(i, carry):
+                at = pl.ds(pl.multiple_of(i * TILE, TILE), TILE)
+                gate_v[j % 2, at, :] = (
+                    act_v[j % 2, at, :].astype(jnp.float32)
+                    * on_v[j % 2, at, :].astype(jnp.float32)
+                ).astype(jnp.bfloat16)
+                return carry
+
+            lax.fori_loop(0, lines // TILE, multiply, 0)
+            store_gate(j).start()
 
     def partner(stage):
         axis, bit = stages[stage]
@@ -189,12 +254,12 @@
 
     first = remote(dir_ref.at[other], pair_in, pair_sem.at[0], pair_sem.at[1], pair)
     values_sent = gather(0, w_value, w_full.at[:, own_columns, :])
+    beside(0)
     first.wait()
     start = dir_ref[mine] + pair_in[...]
     size = half // pieces
     for p in range(pieces):
         acc[0, p] = start[:, p * size : (p + 1) * size]
-    coefficients_sent = []
     for k in range(count):
         copies = []
         for p in range(pieces):
@@ -207,11 +272,7 @@
                     partner((k + p) % count),
                 )
             )
-        if k == 0:
-            load_attn.wait()
-            place_coefficients(pos, attn_v, inv_rms, ct_own)
-            coefficients_sent = gather(1, ct_own, ct_all.at[mp])
-            ct_all[mp] = ct_own[...]
+        beside(k + 1)
         for p in range(pieces):
             copies[p].wait()
             acc[k + 1, p] = acc[k, p] + got[k, p]
@@ -220,6 +281,8 @@
     last = remote(
         dir_full.at[mine], dir_full.at[mine], full_sem.at[0], full_sem.at[1], pair
     )
+    load_attn.start()
+    beside(count + 1)
     load_out.wait()
     last.wait()
 
@@ -238,13 +301,10 @@
         u_all[mp, l] = own_u[:, l * head_size : (l + 1) * head_size]
     u_sent = gather(2, u_all.at[mp], u_all.at[mp])
 
-    for copy in coefficients_sent:
-        copy.wait()
-    delta = target_rows(pos, targets, inv_rms.shape[1])
-    coefficients = jnp.concatenate(
-        [ct_all[m].astype(jnp.float32) for m in range(n_mp)] + [delta] * 2, axis=0
-    )
-    c_ref[...] = coefficients.T.astype(jnp.bfloat16)
+    load_attn.wait()
+    place_coefficients(pos, attn_v, inv_rms, ct_own)
+    coefficients_sent = gather(1, ct_own, ct_all.at[mp])
+    ct_all[mp] = ct_own[...]
     load_value.wait()
     for copy in values_sent:
         copy.wait()
@@ -266,20 +326,57 @@
         )
 
 
-def gate_kernel(straight, c_ref, lower, dec, act_ref, on_ref, out_ref):
-    rank_rows = lower.shape[0]
-    top_row = rank_rows - straight
-    bottom = lax.dot_general(dec[0], lower[...], NT, preferred_element_type=jnp.float32)
-    top = lax.dot_general(
-        dec[1], lower[pl.ds(top_row, straight), :], NT, preferred_element_type=jnp.float32
-    )
-    both = bottom[:, top_row:] + top
-    high = both.astype(jnp.bfloat16).astype(jnp.float32)
-    lane = lax.broadcasted_iota(jnp.int32, both.shape, 1)
-    low = jnp.where(lane < straight // 2, high, both - high)
-    z = jnp.concatenate([bottom[:, :top_row], low], axis=1).astype(jnp.bfloat16)
-    scores = lax.dot_general(c_ref[...], z, NT, preferred_element_type=jnp.float32)
-    out_ref[...] = act_ref[...].astype(jnp.float32) * on_ref[...].astype(jnp.float32) * scores
+    straight = 2 * targets
+    top_row = heads * targets
+    lane = lax.broadcasted_iota(jnp.int32, (chunk, straight), 1)
+
+    def store_z(i):
+        at = pl.ds(pl.multiple_of(i * chunk, chunk), chunk)
+        return pltpu.make_async_copy(z_v.at[at, :], z_ref.at[at, :], z_sem.at[i])
+
+    def score(i, carry):
+        at = pl.ds(pl.multiple_of(i * chunk, chunk), chunk)
+        load_dec(0, i).wait()
+        load_dec(1, i).wait()
+        bottom = lax.dot_general(
+            dec_v[0, at, :], lower[...], NT, preferred_element_type=jnp.float32
+        )
+        top = lax.dot_general(
+            dec_v[1, at, :],
+            lower[pl.ds(top_row, straight), :],
+            NT,
+            preferred_element_type=jnp.float32,
+        )
+        z_v[at, pl.ds(0, top_row)] = bottom[:, :top_row].astype(jnp.bfloat16)
+        both = bottom[:, top_row:] + top
+        high = both.astype(jnp.bfloat16).astype(jnp.float32)
+        z_v[at, pl.ds(top_row, straight)] = jnp.where(
+            lane < targets, high, both - high
+        ).astype(jnp.bfloat16)
+        store_z(i).start()
+        return carry
+
+    lax.fori_loop(0, chunks, score, 0)
+    for copy in coefficients_sent:
+        copy.wait()
+    delta = target_rows(pos, targets, inv_rms.shape[1])
+    coefficients = jnp.concatenate(
+        [ct_all[m].astype(jnp.float32) for m in range(n_mp)] + [delta] * 2, axis=0
+    )
+    c_ref[...] = coefficients.T.astype(jnp.bfloat16)
+    for j in range(max(parts - 2, 0), parts):
+        store_gate(j).wait()
+
+    def drain(i, carry):
+        store_z(i).wait()
+        return carry
+
+    lax.fori_loop(0, chunks, drain, 0)
+
+
+def gate_kernel(c_ref, z_ref, gate_ref, out_ref):
+    scores = lax.dot_general(c_ref[...], z_ref[...], NT, preferred_element_type=jnp.float32)
+    out_ref[...] = gate_ref[...].astype(jnp.float32) * scores
 
 
 def on_device(
@@ -339,15 +436,27 @@
     pieces = 3 if half % (3 * 128) == 0 else 1
     size = half // pieces
     dma = pltpu.SemaphoreType.DMA
-    lower, c = pl.pallas_call(
-        functools.partial(share_kernel, n_mp, n_feat),
+    chunk = chunk_of(features, 512)
+    parts = max(
+        n for n in range(1, steps + 3) if total % n == 0 and (total // n) % TILE == 0
+    )
+    lines = total // parts
+    z, gate, c = pl.pallas_call(
+        functools.partial(share_kernel, n_mp, n_feat, chunk),
         out_shape=(
-            jax.ShapeDtypeStruct((rank_rows, width), bf16),
+            jax.ShapeDtypeStruct((features, rank_rows), bf16),
+            jax.ShapeDtypeStruct((total, features), bf16),
             jax.ShapeDtypeStruct((total, rank_rows), bf16),
         ),
-        in_specs=[smem, vmem, hbm, vmem, vmem, hbm, hbm],
-        out_specs=(vmem, vmem),
+        in_specs=[smem, vmem, hbm, vmem, vmem, hbm, hbm, hbm, hbm, hbm],
+        out_specs=(hbm, hbm, vmem),
         scratch_shapes=[
+            pltpu.VMEM((rank_rows, width), bf16),
+            pltpu.VMEM(decoder.shape, bf16),
+            pltpu.VMEM((features, rank_rows), bf16),
+            pltpu.VMEM((2, lines, features), bf16),
+            pltpu.VMEM((2, lines, features), jnp.int32),
+            pltpu.VMEM((2, lines, features), bf16),
             pltpu.VMEM((targets, half), bf16),
             pltpu.VMEM((steps + 1, pieces, targets, size), bf16),
             pltpu.VMEM((steps, pieces, targets, size), bf16),
@@ -365,6 +474,10 @@
             dma((3,)),
             dma((3, n_mp - 1)),
             dma((3, n_mp - 1)),
+            dma((2, features // chunk)),
+            dma((features // chunk,)),
+            dma((2, parts)),
+            dma((parts,)),
         ],
         compiler_params=pltpu.CompilerParams(
             collective_id=0, has_side_effects=True, vmem_limit_bytes=63 * 2**20
@@ -375,29 +488,38 @@
             transcendentals=0,
         ),
         name="share",
-    )(target_pos, direction, attn_weights, inv_rms, norm_gain, w_out, w_value)
-
-    chunk = chunk_of(features, 384)
+    )(
+        target_pos,
+        direction,
+        attn_weights,
+        inv_rms,
+        norm_gain,
+        w_out,
+        w_value,
+        decoder,
+        activation.reshape(total, features),
+        active.reshape(total, features),
+    )
+
+    block = chunk_of(features, 384)
     out = pl.pallas_call(
-        functools.partial(gate_kernel, 2 * targets),
-        grid=(features // chunk,),
+        gate_kernel,
+        grid=(features // block,),
         out_shape=jax.ShapeDtypeStruct((total, features), f32),
         in_specs=[
             pl.BlockSpec((total, rank_rows), lambda i: (0, 0)),
-            pl.BlockSpec((rank_rows, width), lambda i: (0, 0)),
-            pl.BlockSpec((2, chunk, width), lambda i: (0, i, 0)),
-            pl.BlockSpec((total, chunk), lambda i: (0, i)),
-            pl.BlockSpec((total, chunk), lambda i: (0, i)),
+            pl.BlockSpec((block, rank_rows), lambda i: (i, 0)),
+            pl.BlockSpec((total, block), lambda i: (0, i)),
         ],
-        out_specs=pl.BlockSpec((total, chunk), lambda i: (0, i)),
+        out_specs=pl.BlockSpec((total, block), lambda i: (0, i)),
         compiler_params=pltpu.CompilerParams(vmem_limit_bytes=63 * 2**20),
         cost_estimate=pl.CostEstimate(
-            flops=2 * features * (width + total) * rank_rows,
-            bytes_accessed=10 * total * features + 4 * features * width,
+            flops=2 * features * total * rank_rows,
+            bytes_accessed=6 * total * features,
             transcendentals=0,
         ),
-        name="score_and_gate",
-    )(c, lower, decoder, activation.reshape(total, features), active.reshape(total, features))
+        name="gate",
+    )(c, z, gate)
     return out.reshape(targets, positions, features)
 
 

time: 50.1 us -> 49.5 us (0.988)
  Pallas kernels: 49.9 us -> 49.1 us
    pallas_call x2, Pallas kernels: 45.9 us -> 45.2 us  [the longest x1 35.4 us: on_device(): pl.pallas_call(functools.partial(share_kernel, n_mp, n_feat, chunk), out_...]
where the time goes in v2:
time: 49.5 us; the launch traced here: 49.1 us
  Pallas kernels  49.1 us (99%)
    pallas_call x1, Pallas kernels, on_device(): pl.pallas_call(functools.partial(share_kernel, n_mp, n_feat, chunk), out_...  35.4 us
    pallas_call x1, Pallas kernels, on_device(): pl.pallas_call(gate_kernel, grid=(features // block,), out_shape=jax.Shap...  9.83 us
    pallas_call x1, Pallas kernels, on_device(): pl.pallas_call(pick_kernel, out_shape=jax.ShapeDtypeStruct((2, targets, h...  3.88 us

profile of v2, /device:TPU:0, one launch (start us, length us, event | category | flops | bytes accessed | tf_op | source)
XLA Modules:
  0.0 49.1 jit_solution(17590168039280249792)
XLA Ops:
  0.0 3.9 %pick_rows.1.dir_ref = bf16[2,16,1152]{2,1,0:T(8,128)(2,1)} custom-call(s32[16]{0:T(128)} %ids.1, bf16[4000,2304]{1,0:T(8,128)(2,1)} %unembed.1), custom_call_target="tpu_custom_call" | custom-call | flops 18874368 | bytes 1179648 | tf_op jit(solution)/shard_map/pick_rows/pallas_call | solution.py:417
  3.9 35.4 %share.1 = (bf16[3072,160]{1,0:T(8,128)(2,1)}, bf16[768,3072]{1,0:T(8,128)(2,1)}, bf16[768,160]{1,0:T(8,128)(2,1)}) custom-call(s32[16]{0:T(128)} %pos.1, bf16[2,16,1152]{2,1,0:T(8,128)(2,1)} %pick_rows.1.dir_ref, f32[4,16,48,48]{3,2,1,0:T(8,128)} %attn.1, f32[16,48]{1,0:T(8,128)} %inv_rms.1, f32[2304]{0:T(1024)} %gain_ref.1, bf16[4,256,2304]{2,1,0:T(8,128)(2,1)} %w_out.1, ...), custom_call_target="tpu_custom_call" | custom-call | flops 2264924160 | bytes 42467328 | tf_op jit(solution)/shard_map/share/pallas_call | solution.py:444
  39.3 9.8 %gate.1 = f32[768,3072]{1,0:T(8,128)} custom-call(bf16[768,160]{1,0:T(8,128)(2,1)} %get-tuple-element.8.c_ref, bf16[3072,160]{1,0:T(8,128)(2,1)} %get-tuple-element.9.z_ref, bf16[768,3072]{1,0:T(8,128)(2,1)} %get-tuple-element.10.gate_ref), custom_call_target="tpu_custom_call" | custom-call | flops 754974720 | bytes 14155776 | tf_op jit(solution)/shard_map/gate/pallas_call | solution.py:505

commit v3 on v2

--- a/solution.py
+++ b/solution.py
@@ -24,7 +24,9 @@
     return max(c for c in range(TILE, most + 1, TILE) if n % c == 0)
 
 
-def pick_kernel(ids, unembed, dir_ref, blocks, sems):
+def pick_kernel(
+    ids, pos, unembed, attn, inv_rms, dir_ref, ct_ref, delta_ref, blocks, attn_v, sems, attn_sem
+):
     rows, width = unembed.shape
     targets = dir_ref.shape[1]
     half = width // 2
@@ -42,6 +44,9 @@
 
     for g in range(targets):
         fetch(g).start()
+    load_attn = pltpu.make_async_copy(attn, attn_v, attn_sem)
+    load_attn.start()
+    delta_ref[...] = target_rows(pos, targets, inv_rms.shape[1]).astype(jnp.bfloat16)
     lane = lax.broadcasted_iota(jnp.int32, (targets, targets * TILE), 1)
     row = lax.broadcasted_iota(jnp.int32, (targets, targets * TILE), 0)
     picker = jnp.zeros((targets, targets * TILE), jnp.float32)
@@ -57,6 +62,8 @@
         dir_ref[c] = jnp.dot(
             picker, blocks[:, pl.ds(c * half, half)], preferred_element_type=jnp.float32
         ).astype(jnp.bfloat16)
+    load_attn.wait()
+    place_coefficients(pos, attn_v, inv_rms, ct_ref)
 
 
 def place_coefficients(pos, attn, inv_rms, ct_ref):
@@ -104,10 +111,9 @@
     n_mp,
     n_feat,
     chunk,
-    pos,
     dir_ref,
-    attn,
-    inv_rms,
+    ct_ref,
+    delta_ref,
     gain_ref,
     w_out,
     w_value,
@@ -127,12 +133,11 @@
     acc,
     got,
     dir_full,
-    attn_v,
     w_out_v,
     w_full,
     u_all,
-    ct_own,
     ct_all,
+    d_top,
     pair_sem,
     step_send,
     step_recv,
@@ -160,7 +165,6 @@
     heads = local_heads * n_mp
 
     own_columns = pl.ds(pl.multiple_of(mp * columns, TILE), columns)
-    load_attn = pltpu.make_async_copy(attn, attn_v, w_sem.at[2])
     load_out = pltpu.make_async_copy(w_out, w_out_v, w_sem.at[0])
     load_value = pltpu.make_async_copy(w_value, w_full.at[:, own_columns, :], w_sem.at[1])
     load_out.start()
@@ -253,6 +257,7 @@
         ]
 
     first = remote(dir_ref.at[other], pair_in, pair_sem.at[0], pair_sem.at[1], pair)
+    coefficients_sent = gather(1, ct_ref, ct_all.at[mp])
     values_sent = gather(0, w_value, w_full.at[:, own_columns, :])
     beside(0)
     first.wait()
@@ -281,8 +286,16 @@
     last = remote(
         dir_full.at[mine], dir_full.at[mine], full_sem.at[0], full_sem.at[1], pair
     )
-    load_attn.start()
     beside(count + 1)
+    ct_all[mp] = ct_ref[...]
+    for copy in coefficients_sent:
+        copy.wait()
+    coefficients = jnp.concatenate(
+        [ct_all[m].astype(jnp.float32) for m in range(n_mp)]
+        + [delta_ref[...].astype(jnp.float32)] * 2,
+        axis=0,
+    )
+    c_ref[...] = coefficients.T.astype(jnp.bfloat16)
     load_out.wait()
     last.wait()
 
@@ -301,10 +314,22 @@
         u_all[mp, l] = own_u[:, l * head_size : (l + 1) * head_size]
     u_sent = gather(2, u_all.at[mp], u_all.at[mp])
 
-    load_attn.wait()
-    place_coefficients(pos, attn_v, inv_rms, ct_own)
-    coefficients_sent = gather(1, ct_own, ct_all.at[mp])
-    ct_all[mp] = ct_own[...]
+    straight = 2 * targets
+    top_row = heads * targets
+
+    def top(i, carry):
+        at = pl.ds(pl.multiple_of(i * chunk, chunk), chunk)
+        load_dec(1, i).wait()
+        d_top[at, :] = lax.dot_general(
+            dec_v[1, at, :],
+            lower[pl.ds(top_row, straight), :],
+            NT,
+            preferred_element_type=jnp.float32,
+        )
+        return carry
+
+    early = chunks // 2
+    lax.fori_loop(0, early, top, 0)
     load_value.wait()
     for copy in values_sent:
         copy.wait()
@@ -326,8 +351,7 @@
         )
 
 
-    straight = 2 * targets
-    top_row = heads * targets
+    lax.fori_loop(early, chunks, top, 0)
     lane = lax.broadcasted_iota(jnp.int32, (chunk, straight), 1)
 
     def store_z(i):
@@ -337,18 +361,11 @@
     def score(i, carry):
         at = pl.ds(pl.multiple_of(i * chunk, chunk), chunk)
         load_dec(0, i).wait()
-        load_dec(1, i).wait()
         bottom = lax.dot_general(
             dec_v[0, at, :], lower[...], NT, preferred_element_type=jnp.float32
         )
-        top = lax.dot_general(
-            dec_v[1, at, :],
-            lower[pl.ds(top_row, straight), :],
-            NT,
-            preferred_element_type=jnp.float32,
-        )
         z_v[at, pl.ds(0, top_row)] = bottom[:, :top_row].astype(jnp.bfloat16)
-        both = bottom[:, top_row:] + top
+        both = bottom[:, top_row:] + d_top[at, :]
         high = both.astype(jnp.bfloat16).astype(jnp.float32)
         z_v[at, pl.ds(top_row, straight)] = jnp.where(
             lane < targets, high, both - high
@@ -357,13 +374,6 @@
         return carry
 
     lax.fori_loop(0, chunks, score, 0)
-    for copy in coefficients_sent:
-        copy.wait()
-    delta = target_rows(pos, targets, inv_rms.shape[1])
-    coefficients = jnp.concatenate(
-        [ct_all[m].astype(jnp.float32) for m in range(n_mp)] + [delta] * 2, axis=0
-    )
-    c_ref[...] = coefficients.T.astype(jnp.bfloat16)
     for j in range(max(parts - 2, 0), parts):
         store_gate(j).wait()
 
@@ -414,14 +424,20 @@
         local = target_ids - rank * vocab_rows
         inside = (local >= 0) & (local < vocab_rows)
         target_ids = jnp.where(inside, rank * unembed.shape[0] + local, -1)
-    direction = pl.pallas_call(
+    direction, coefficients, delta = pl.pallas_call(
         pick_kernel,
-        out_shape=jax.ShapeDtypeStruct((2, targets, half), bf16),
-        in_specs=[smem, hbm],
-        out_specs=vmem,
+        out_shape=(
+            jax.ShapeDtypeStruct((2, targets, half), bf16),
+            jax.ShapeDtypeStruct((local_heads * targets, total), bf16),
+            jax.ShapeDtypeStruct((targets, total), bf16),
+        ),
+        in_specs=[smem, smem, hbm, hbm, vmem],
+        out_specs=(vmem, vmem, vmem),
         scratch_shapes=[
             pltpu.VMEM((targets * TILE, width), bf16),
+            pltpu.VMEM(attn_weights.shape, f32),
             pltpu.SemaphoreType.DMA((targets,)),
+            pltpu.SemaphoreType.DMA,
         ],
         compiler_params=pltpu.CompilerParams(vmem_limit_bytes=63 * 2**20),
         cost_estimate=pl.CostEstimate(
@@ -430,7 +446,7 @@
             transcendentals=0,
         ),
         name="pick_rows",
-    )(target_ids, unembed)
+    )(target_ids, target_pos, unembed, attn_weights, inv_rms)
 
     steps = len(bits_of(n_feat)) + len(bits_of(n_mp)) - 1
     pieces = 3 if half % (3 * 128) == 0 else 1
@@ -448,7 +464,7 @@
             jax.ShapeDtypeStruct((total, features), bf16),
             jax.ShapeDtypeStruct((total, rank_rows), bf16),
         ),
-        in_specs=[smem, vmem, hbm, vmem, vmem, hbm, hbm, hbm, hbm, hbm],
+        in_specs=[vmem, vmem, vmem, vmem, hbm, hbm, hbm, hbm, hbm],
         out_specs=(hbm, hbm, vmem),
         scratch_shapes=[
             pltpu.VMEM((rank_rows, width), bf16),
@@ -461,17 +477,16 @@
             pltpu.VMEM((steps + 1, pieces, targets, size), bf16),
             pltpu.VMEM((steps, pieces, targets, size), bf16),
             pltpu.VMEM((2, targets, half), bf16),
-            pltpu.VMEM(attn_weights.shape, f32),
             pltpu.VMEM(w_out.shape, bf16),
             pltpu.VMEM((kv_heads, columns * n_mp, head_size), bf16),
             pltpu.VMEM((n_mp, local_heads, targets, head_size), bf16),
-            pltpu.VMEM((local_heads * targets, total), bf16),
             pltpu.VMEM((n_mp, local_heads * targets, total), bf16),
+            pltpu.VMEM((features, 2 * targets), f32),
             dma((2,)),
             dma((steps, pieces)),
             dma((steps, pieces)),
             dma((2,)),
-            dma((3,)),
+            dma((2,)),
             dma((3, n_mp - 1)),
             dma((3, n_mp - 1)),
             dma((2, features // chunk)),
@@ -489,10 +504,9 @@
         ),
         name="share",
     )(
-        target_pos,
         direction,
-        attn_weights,
-        inv_rms,
+        coefficients,
+        delta,
         norm_gain,
         w_out,
         w_value,
@@ -501,7 +515,7 @@
         active.reshape(total, features),
     )
 
-    block = chunk_of(features, 384)
+    block = chunk_of(features, 768)
     out = pl.pallas_call(
         gate_kernel,
         grid=(features // block,),

time: 49.5 us -> 48 us (0.970)
  Pallas kernels: 49.1 us -> 47.7 us
    pallas_call x1, Pallas kernels: 9.83 us -> 7.64 us  [on_device(): pl.pallas_call(gate_kernel, grid=(features // block,), out_shape=jax.Shap...]
    pallas_call x1, Pallas kernels: 3.88 us -> 5.19 us  [on_device(): pl.pallas_call(pick_kernel, out_shape=(jax.ShapeDtypeStruct((2, targets,...]
    pallas_call x1, Pallas kernels: 35.4 us -> 34.8 us  [on_device(): pl.pallas_call(functools.partial(share_kernel, n_mp, n_feat, chunk), out_...]
where the time goes in v3:
time: 48 us; the launch traced here: 47.7 us
  Pallas kernels  47.7 us (99%)
    pallas_call x1, Pallas kernels, on_device(): pl.pallas_call(functools.partial(share_kernel, n_mp, n_feat, chunk), out_...  34.8 us
    pallas_call x1, Pallas kernels, on_device(): pl.pallas_call(gate_kernel, grid=(features // block,), out_shape=jax.Shap...  7.64 us
    pallas_call x1, Pallas kernels, on_device(): pl.pallas_call(pick_kernel, out_shape=(jax.ShapeDtypeStruct((2, targets,...  5.19 us

profile of v3, /device:TPU:0, one launch (start us, length us, event | category | flops | bytes accessed | tf_op | source)
XLA Modules:
  0.0 47.7 jit_solution(3659226275488198533)
XLA Ops:
  0.0 5.2 %pick_rows.1 = (bf16[2,16,1152]{2,1,0:T(8,128)(2,1)}, bf16[64,768]{1,0:T(8,128)(2,1)}, bf16[16,768]{1,0:T(8,128)(2,1)}) custom-call(s32[16]{0:T(128)} %ids.1, s32[16]{0:T(128)} %pos.1, bf16[4000,2304]{1,0:T(8,128)(2,1)} %unembed.1, f32[4,16,48,48]{3,2,1,0:T(8,128)} %attn.1, f32[16,48]{1,0:T(8,128)} %inv_rms.1), custom_call_target="tpu_custom_call" | custom-call | flops 18874368 | bytes 1179648 | tf_op jit(solution)/shard_map/pick_rows/pallas_call | solution.py:427
  5.2 34.8 %share.1 = (bf16[3072,160]{1,0:T(8,128)(2,1)}, bf16[768,3072]{1,0:T(8,128)(2,1)}, bf16[768,160]{1,0:T(8,128)(2,1)}) custom-call(bf16[2,16,1152]{2,1,0:T(8,128)(2,1)} %get-tuple-element.11.dir_ref, bf16[64,768]{1,0:T(8,128)(2,1)} %get-tuple-element.12.ct_ref, bf16[16,768]{1,0:T(8,128)(2,1)} %get-tuple-element.13.delta_ref, f32[2304]{0:T(1024)} %gain_ref.1, ...), custom_call_target="tpu_custom_call" | custom-call | flops 2264924160 | bytes 42467328 | tf_op jit(solution)/shard_map/share/pallas_call | solution.py:460
  40.0 7.6 %gate.1 = f32[768,3072]{1,0:T(8,128)} custom-call(bf16[768,160]{1,0:T(8,128)(2,1)} %get-tuple-element.14.c_ref, bf16[3072,160]{1,0:T(8,128)(2,1)} %get-tuple-element.15.z_ref, bf16[768,3072]{1,0:T(8,128)(2,1)} %get-tuple-element.16.gate_ref), custom_call_target="tpu_custom_call" | custom-call | flops 754974720 | bytes 14155776 | tf_op jit(solution)/shard_map/gate/pallas_call | solution.py:519

commit v4 on v3

--- a/solution.py
+++ b/solution.py
@@ -328,8 +328,7 @@
         )
         return carry
 
-    early = chunks // 2
-    lax.fori_loop(0, early, top, 0)
+    lax.fori_loop(0, chunks, top, 0)
     load_value.wait()
     for copy in values_sent:
         copy.wait()
@@ -351,7 +350,6 @@
         )
 
 
-    lax.fori_loop(early, chunks, top, 0)
     lane = lax.broadcasted_iota(jnp.int32, (chunk, straight), 1)
 
     def store_z(i):
@@ -452,7 +450,7 @@
     pieces = 3 if half % (3 * 128) == 0 else 1
     size = half // pieces
     dma = pltpu.SemaphoreType.DMA
-    chunk = chunk_of(features, 512)
+    chunk = chunk_of(features, 1024)
     parts = max(
         n for n in range(1, steps + 3) if total % n == 0 and (total // n) % TILE == 0
     )

time: 48 us -> 47.3 us (0.985)
  Pallas kernels: 47.7 us -> 47.1 us
    pallas_call x1, Pallas kernels: 34.8 us -> 34.2 us  [on_device(): pl.pallas_call(functools.partial(share_kernel, n_mp, n_feat, chunk), out_...]
where the time goes in v4:
time: 47.3 us; the launch traced here: 47.1 us
  Pallas kernels  47.1 us (100%)
    pallas_call x1, Pallas kernels, on_device(): pl.pallas_call(functools.partial(share_kernel, n_mp, n_feat, chunk), out_...  34.2 us
    pallas_call x1, Pallas kernels, on_device(): pl.pallas_call(gate_kernel, grid=(features // block,), out_shape=jax.Shap...  7.65 us
    pallas_call x1, Pallas kernels, on_device(): pl.pallas_call(pick_kernel, out_shape=(jax.ShapeDtypeStruct((2, targets,...  5.19 us

profile of v4, /device:TPU:0, one launch (start us, length us, event | category | flops | bytes accessed | tf_op | source)
XLA Modules:
  0.0 47.1 jit_solution(3442276984286524568)
XLA Ops:
  0.0 5.2 %pick_rows.1 = (bf16[2,16,1152]{2,1,0:T(8,128)(2,1)}, bf16[64,768]{1,0:T(8,128)(2,1)}, bf16[16,768]{1,0:T(8,128)(2,1)}) custom-call(s32[16]{0:T(128)} %ids.1, s32[16]{0:T(128)} %pos.1, bf16[4000,2304]{1,0:T(8,128)(2,1)} %unembed.1, f32[4,16,48,48]{3,2,1,0:T(8,128)} %attn.1, f32[16,48]{1,0:T(8,128)} %inv_rms.1), custom_call_target="tpu_custom_call" | custom-call | flops 18874368 | bytes 1179648 | tf_op jit(solution)/shard_map/pick_rows/pallas_call | solution.py:425
  5.2 34.2 %share.1 = (bf16[3072,160]{1,0:T(8,128)(2,1)}, bf16[768,3072]{1,0:T(8,128)(2,1)}, bf16[768,160]{1,0:T(8,128)(2,1)}) custom-call(bf16[2,16,1152]{2,1,0:T(8,128)(2,1)} %get-tuple-element.11.dir_ref, bf16[64,768]{1,0:T(8,128)(2,1)} %get-tuple-element.12.ct_ref, bf16[16,768]{1,0:T(8,128)(2,1)} %get-tuple-element.13.delta_ref, f32[2304]{0:T(1024)} %gain_ref.1, ...), custom_call_target="tpu_custom_call" | custom-call | flops 2264924160 | bytes 42467328 | tf_op jit(solution)/shard_map/share/pallas_call | solution.py:458
  39.4 7.6 %gate.1 = f32[768,3072]{1,0:T(8,128)} custom-call(bf16[768,160]{1,0:T(8,128)(2,1)} %get-tuple-element.14.c_ref, bf16[3072,160]{1,0:T(8,128)(2,1)} %get-tuple-element.15.z_ref, bf16[768,3072]{1,0:T(8,128)(2,1)} %get-tuple-element.16.gate_ref), custom_call_target="tpu_custom_call" | custom-call | flops 754974720 | bytes 14155776 | tf_op jit(solution)/shard_map/gate/pallas_call | solution.py:517
